TPU v7x, 32 devices: a whole 2x2x4 slice. The times are simulated.
32 devices in a mesh: groups: 2 (over x), slab: 16 (over z, y, core).
Axes of the slice: x: 2, y: 2, z: 4, core: 2. Of those that a mesh axis runs over, the one named last changes fastest.
Arguments:
- mode_shapes: float32 [16384, 192], P(('groups', 'slab')), parts along dimension 0, may hold values from -6 to 6
- wall_coupling: float32 [16384, 15], P(('groups', 'slab')), parts along dimension 0, may hold values from -3.5 to 3.5
- owner_dev: int32 [16384, 1], P(('groups', 'slab')), parts along dimension 0, may hold values from 0 to 15; in each aligned block of 512 rows (0 to 511, 512 to 1023, ...) at most 64 rows name the same one
- owner_cell: int32 [16384], P(('groups', 'slab')), parts along dimension 0, may hold values from 0 to 2047
- neighbours: int32 [6, 65536], P(None, ('groups', 'slab')), parts along dimension 1, may hold values from -1 to 32767, as said below
- coupling_blocks: float32 [6, 5, 5, 65536], P(None, None, None, ('groups', 'slab')), parts along dimension 3, may hold values from -0.3 to 0.3
- inv_blocks: float32 [5, 5, 65536], P(None, None, ('groups', 'slab')), parts along dimension 2, may hold values from -0.9 to 3, as said below
Outputs:
- modes_basis: float32 [5, 64, 65536], P(None, None, ('groups', 'slab')), parts along dimension 2
- factor: float32 [128, 64], P('groups'), parts along dimension 0
There are 2 independent parts, one for each index of `groups`. A program takes and returns all parts, laid end to end along the dimension named above; each array names one. Nothing has to cross between parts.
Inputs may be any that keep to these rules, and one draw needn't show every extreme that they name: `owner_dev`: in the rows of one slab device at most 64 shell nodes name the same slab, a bound that some of them reach. `neighbours`: A filled slot of cell c names a cell whose number differs from c by 1 to 256. `inv_blocks`: each block has a positive diagonal entry shared by its five diagonal places and off-diagonal entries of at most 0.3 times it in magnitude.
All inputs are finite; a program needn't handle non-finite values.
Results may differ from a plain program's by a relative error of at most 0.0003.
Values sent between devices are 32-bit elements; how exact they have to be, the bound alone decides.
No kernel may reach another device: no remote copies, remote signals or barrier semaphores. Data moves between devices by JAX's collectives and lax.ppermute only.
A program may use at most 192 MiB of HBM per device.

v0:
```python
import math
import jax
import jax.numpy as jnp
from jax import lax
from jax.sharding import PartitionSpec as P

VARS = 5
NBR = 6
SWEEPS = 2


def with_halo(x, sides, width):
    for axis, dim in sides:
        count, length = (lax.axis_size(axis), x.shape[dim])
        up = [(i, (i + 1) % count) for i in range(count - 1)]
        down = [(j, i) for i, j in up]
        last = lax.slice_in_dim(x, length - width, length, axis=dim)
        first = lax.slice_in_dim(x, 0, width, axis=dim)
        before = lax.ppermute(last, axis, up)
        after = lax.ppermute(first, axis, down)
        x = jnp.concatenate([before, x, after], axis=dim)
    return x


def apply_blocks(blocks, field_in):
    rows_out = []
    for out_var in range(field_in.shape[0]):
        summed = blocks[out_var, 0][None, :] * field_in[0]
        for in_var in range(1, field_in.shape[0]):
            summed = summed + blocks[out_var, in_var][None, :] * field_in[in_var]
        rows_out.append(summed)
    return jnp.stack(rows_out)


def couple(weights, shapes):
    node_count = weights.shape[0]
    modes_total = shapes.shape[1] // 3
    weights_split = weights.reshape(node_count, -1, 3)
    shapes_split = shapes.reshape(node_count, 3, modes_total)
    summed = weights_split[:, :, 0, None] * shapes_split[:, None, 0, :]
    for component in range(1, 3):
        summed = summed + weights_split[:, :, component, None] * shapes_split[:, None, component, :]
    return summed.reshape(node_count, -1)


def gram_matrix(left_field, right_field):
    return jnp.einsum("vpc,vqc->pq", left_field, right_field, precision=lax.Precision.HIGHEST)


def combine(coeffs, field_in):
    return jnp.einsum("pq,vpc->vqc", coeffs, field_in, precision=lax.Precision.HIGHEST)


def cholesky_upper(gram):
    order = gram.shape[0]
    places = jnp.arange(order, dtype=jnp.int32)

    def column_step(column_at, lower):
        row_now = lax.dynamic_index_in_dim(lower, column_at, 0, keepdims=False)
        target = lax.dynamic_index_in_dim(gram, column_at, 1, keepdims=False)
        reduced = target - jnp.dot(lower, row_now, precision=lax.Precision.HIGHEST)
        pivot = jnp.sqrt(lax.dynamic_index_in_dim(reduced, column_at, 0, keepdims=False))
        column = jnp.where(
            places > column_at, reduced / pivot, jnp.where(places == column_at, pivot, 0.0)
        )
        return jnp.where(places[None, :] == column_at, column[:, None], lower)

    lower = lax.fori_loop(0, order, column_step, jnp.zeros((order, order), jnp.float32))
    return lower.T


def upper_inverse(upper):
    lower = upper.T
    order = lower.shape[0]
    places = jnp.arange(order, dtype=jnp.int32)
    identity = jnp.eye(order, dtype=jnp.float32)

    def row_step(row_at, inverse):
        lower_row = lax.dynamic_index_in_dim(lower, row_at, 0, keepdims=False)
        pivot = lax.dynamic_index_in_dim(lower_row, row_at, 0, keepdims=False)
        earlier = jnp.where(places < row_at, lower_row, 0.0)
        unit_row = lax.dynamic_index_in_dim(identity, row_at, 0, keepdims=False)
        new_row = (unit_row - jnp.dot(earlier, inverse, precision=lax.Precision.HIGHEST)) / pivot
        return jnp.where(places[:, None] == row_at, new_row[None, :], inverse)

    inverse = lax.fori_loop(0, order, row_step, jnp.zeros((order, order), jnp.float32))
    return inverse.T


def local(
    mode_shapes, wall_coupling, owner_dev, owner_cell, neighbours, coupling_blocks, inv_blocks
):
    devices_slab = lax.axis_size("slab")
    cell_count = inv_blocks.shape[2]
    node_count = mode_shapes.shape[0]
    modes_total = mode_shapes.shape[1] // 3
    capacity = max(2, 2 * node_count // devices_slab)
    destination = owner_dev[:, 0]
    onehot_dest = (
        destination[:, None] == jnp.arange(devices_slab, dtype=jnp.int32)[None, :]
    ).astype(jnp.int32)
    ranking = jnp.sum((jnp.cumsum(onehot_dest, axis=0) - 1) * onehot_dest, axis=1)
    slot_of = destination * capacity + ranking
    slot_total = devices_slab * capacity
    cell_tags = (
        jnp.full((slot_total,), -1.0, jnp.float32).at[slot_of].set(owner_cell.astype(jnp.float32))
    )
    contribution = couple(wall_coupling, mode_shapes)
    outgoing = (
        jnp.zeros((slot_total, contribution.shape[1]), jnp.float32).at[slot_of].set(contribution)
    )
    arrived, arrived_tags = (
        lax.all_to_all(outgoing, "slab", split_axis=0, concat_axis=0, tiled=True),
        lax.all_to_all(cell_tags, "slab", split_axis=0, concat_axis=0, tiled=True),
    )
    matches = (
        arrived_tags.astype(jnp.int32)[:, None] == jnp.arange(cell_count, dtype=jnp.int32)[None, :]
    ).astype(jnp.float32)
    forcing = lax.dot_general(
        arrived, matches, (((0,), (0,)), ((), ())), precision=lax.Precision.HIGHEST
    )
    forcing = forcing.reshape(VARS, modes_total, cell_count)
    rim_width = cell_count // 8
    first_cell = lax.axis_index("slab") * cell_count - rim_width
    local_ids = jnp.where(neighbours >= 0, neighbours - first_cell, cell_count + 2 * rim_width)
    state_field = apply_blocks(inv_blocks, forcing)
    for sweep_step in range(SWEEPS):
        widened = with_halo(state_field, (("slab", 2),), rim_width)
        padded = jnp.concatenate(
            [widened, jnp.zeros(widened.shape[:2] + (1,), jnp.float32)], axis=2
        )
        coupled = jnp.zeros_like(state_field)
        for slot_index in range(NBR):
            gathered = jnp.take(padded, local_ids[slot_index], axis=2)
            coupled = coupled + apply_blocks(coupling_blocks[slot_index], gathered)
        state_field = apply_blocks(inv_blocks, forcing - coupled)
    block_width = modes_total // 4
    factor = jnp.zeros((modes_total, modes_total), jnp.float32)
    basis_parts = []
    for block_index in range(4):
        start_col = block_index * block_width
        panel_cols = state_field[:, start_col : start_col + block_width, :]
        if block_index > 0:
            previous = jnp.concatenate(basis_parts, axis=1)
            projection = lax.psum(gram_matrix(previous, panel_cols), "slab")
            panel_cols = panel_cols - combine(projection, previous)
            factor = factor.at[:start_col, start_col : start_col + block_width].set(projection)
        diag_block = cholesky_upper(lax.psum(gram_matrix(panel_cols, panel_cols), "slab"))
        factor = factor.at[
            start_col : start_col + block_width, start_col : start_col + block_width
        ].set(diag_block)
        basis_parts.append(combine(upper_inverse(diag_block), panel_cols))
    basis_out = jnp.concatenate(basis_parts, axis=1)
    norm_scale = math.sqrt(VARS * cell_count * devices_slab)
    return (basis_out * norm_scale, factor / norm_scale)


def solution(mesh):
    in_specs = (
        P(("groups", "slab"), None),
        P(("groups", "slab"), None),
        P(("groups", "slab"), None),
        P(("groups", "slab")),
        P(None, ("groups", "slab")),
        P(None, None, None, ("groups", "slab")),
        P(None, None, ("groups", "slab")),
    )
    out_specs = (P(None, None, ("groups", "slab")), P("groups", None))
    return jax.shard_map(local, mesh=mesh, in_specs=in_specs, out_specs=out_specs, check_vma=False)
```

profile of v0, /device:TPU:0, one launch (start us, length us, event | category | flops | bytes accessed | tf_op | source)
XLA Modules:
  0.0 1054.8 jit_solution(16598022416229044817)
XLA Ops:
  8.1 7.4 all-to-all-start.1
  52.9 27.0 %all-to-all-done = f32[16,64,320]{2,1,0:T(8,128)S(1)} async-done(((f32[16,64,320]{2,1,0:T(8,128)}), f32[16,64,320]{2,1,0:T(8,128)S(1)}, u32[]{:S(2)}, u32[]{:S(2)}) %all-to-all-start) | async-done | bytes 1310752 | tf_op jit(solution)/shard_map/all_to_all | solution.py:113
  98.3 7.6 copy.130
  105.9 19.7 %gather_fusion.5 = f32[2048,5,64]{2,1,0:T(8,128)} fusion(f32[5,64,2561]{1,0,2:T(8,128)} %copy.130, s32[2048]{0:T(1024)} %get-tuple-element.1568), kind=kCustom, calls=%fused_computation.5.clone | custom fusion | bytes 5251072 | tf_op jit(solution)/shard_map/jit(_take)/gather | solution.py:134
  131.7 19.6 %gather_fusion.4 = f32[2048,5,64]{2,1,0:T(8,128)} fusion(f32[5,64,2561]{1,0,2:T(8,128)} %copy.130, s32[2048]{0:T(1024)S(1)} %copy-done.195), kind=kCustom, calls=%fused_computation.4.clone | custom fusion | bytes 5251072 | tf_op jit(solution)/shard_map/jit(_take)/gather | solution.py:134
  157.4 19.6 %gather_fusion.3 = f32[2048,5,64]{2,1,0:T(8,128)} fusion(f32[5,64,2561]{1,0,2:T(8,128)} %copy.130, s32[2048]{0:T(1024)S(1)} %copy-done.193), kind=kCustom, calls=%fused_computation.3.clone | custom fusion | bytes 5251072 | tf_op jit(solution)/shard_map/jit(_take)/gather | solution.py:134
  183.1 19.6 %gather_fusion.2 = f32[2048,5,64]{2,1,0:T(8,128)} fusion(f32[5,64,2561]{1,0,2:T(8,128)} %copy.130, s32[2048]{0:T(1024)S(1)} %copy-done.198), kind=kCustom, calls=%fused_computation.2.clone | custom fusion | bytes 5251072 | tf_op jit(solution)/shard_map/jit(_take)/gather | solution.py:134
  208.8 19.6 %gather_fusion.1 = f32[2048,5,64]{2,1,0:T(8,128)} fusion(f32[5,64,2561]{1,0,2:T(8,128)} %copy.130, s32[2048]{0:T(1024)S(1)} %copy-done.196), kind=kCustom, calls=%fused_computation.1.clone | custom fusion | bytes 5251072 | tf_op jit(solution)/shard_map/jit(_take)/gather | solution.py:134
  234.5 19.6 %gather_fusion = f32[2048,5,64]{2,1,0:T(8,128)} fusion(f32[5,64,2561]{1,0,2:T(8,128)} %copy.130, s32[2048]{0:T(1024)S(1)} %get-tuple-element.1569), kind=kCustom, calls=%fused_computation.clone | custom fusion | bytes 5251072 | tf_op jit(solution)/shard_map/jit(_take)/gather | solution.py:134
  291.8 7.3 collective-permute-start.2
  304.6 7.6 copy.147
  312.3 19.7 %gather_fusion.11 = f32[2048,5,64]{2,1,0:T(8,128)} fusion(f32[5,64,2561]{1,0,2:T(8,128)} %copy.147, s32[2048]{0:T(1024)} %get-tuple-element.1568), kind=kCustom, calls=%fused_computation.11.clone | custom fusion | bytes 5251072 | tf_op jit(solution)/shard_map/jit(_take)/gather | solution.py:134
  332.0 19.8 %gather_fusion.10 = f32[2048,5,64]{2,1,0:T(8,128)} fusion(f32[5,64,2561]{1,0,2:T(8,128)} %copy.147, s32[2048]{0:T(1024)} %get-tuple-element.1567), kind=kCustom, calls=%fused_computation.10.clone | custom fusion | bytes 5251072 | tf_op jit(solution)/shard_map/jit(_take)/gather | solution.py:134
  351.9 19.7 %gather_fusion.9 = f32[2048,5,64]{2,1,0:T(8,128)} fusion(f32[5,64,2561]{1,0,2:T(8,128)} %copy.147, s32[2048]{0:T(1024)S(1)} %copy-done.194), kind=kCustom, calls=%fused_computation.9.clone | custom fusion | bytes 5251072 | tf_op jit(solution)/shard_map/jit(_take)/gather | solution.py:134
  371.5 19.8 %gather_fusion.8 = f32[2048,5,64]{2,1,0:T(8,128)} fusion(f32[5,64,2561]{1,0,2:T(8,128)} %copy.147, s32[2048]{0:T(1024)} %get-tuple-element.1565), kind=kCustom, calls=%fused_computation.8.clone | custom fusion | bytes 5251072 | tf_op jit(solution)/shard_map/jit(_take)/gather | solution.py:134
  391.4 19.8 %gather_fusion.7 = f32[2048,5,64]{2,1,0:T(8,128)} fusion(f32[5,64,2561]{1,0,2:T(8,128)} %copy.147, s32[2048]{0:T(1024)S(1)} %copy-done.197), kind=kCustom, calls=%fused_computation.7.clone | custom fusion | bytes 5251072 | tf_op jit(solution)/shard_map/jit(_take)/gather | solution.py:134
  411.2 19.7 %gather_fusion.6 = f32[2048,5,64]{2,1,0:T(8,128)} fusion(f32[5,64,2561]{1,0,2:T(8,128)} %copy.147, s32[2048]{0:T(1024)} %copy-done.199), kind=kCustom, calls=%fused_computation.6.clone | custom fusion | bytes 5251072 | tf_op jit(solution)/shard_map/jit(_take)/gather | solution.py:134
  511.8 37.7 %psum.49 = f32[16,16]{1,0:T(8,128)S(1)} all-reduce(f32[16,16]{1,0:T(8,128)S(1)} %convolution_bitcast_fusion.20), channel_id=1, replica_groups=mesh['groups'=2,'slab'=16] {'slab'}, use_global_device_ids=true, to_apply=%region_5.7 | all-reduce | flops 256 | bytes 2048 | tf_op jit(solution)/shard_map/psum | solution.py:148
  549.6 24.4 %while.139 = (s32[]{:T(128)}, f32[16,16]{1,0:T(8,128)S(1)}, f32[16,16]{0,1:T(8,128)S(1)}, s32[]{:T(128)}, s32[]{:T(128)}) while((s32[]{:T(128)}, f32[16,16]{1,0:T(8,128)S(1)}, f32[16,16]{0,1:T(8,128)S(1)}, s32[]{:T(128)}, s32[]{:T(128)}) %tuple.552), condition=%wide.region_7.9_spmd.clone.clone, body=%wide.region_6.8_spmd.clone.clone.sunk | while | flops 3955 | bytes 14736 | solution.py:68
  574.0 34.1 %while.140 = (s32[]{:T(128)}, f32[16,16]{1,0:T(8,128)S(1)}, f32[16,16]{1,0:T(8,128)}, f32[16,16]{1,0:T(8,128)S(1)}, s32[]{:T(128)}, /*index=5*/s32[]{:T(128)}, s32[]{:T(128)}) while((s32[]{:T(128)}, f32[16,16]{1,0:T(8,128)S(1)}, f32[16,16]{1,0:T(8,128)}, f32[16,16]{1,0:T(8,128)S(1)}, s32[]{:T(128)}, ...), condition=%wide.region_9.11_spmd.clone.clone, body=%wide.region_8.10_spmd.clone.clone.sunk | while | flops 3924 | bytes 13155 | solution.py:86
  609.8 30.0 %psum.50 = f32[16,16]{1,0:T(8,128)S(1)} all-reduce(f32[16,16]{1,0:T(8,128)S(1)} %convolution_bitcast_fusion.19), channel_id=1, replica_groups=mesh['groups'=2,'slab'=16] {'slab'}, use_global_device_ids=true, to_apply=%region_10.12 | all-reduce | flops 256 | bytes 2048 | tf_op jit(solution)/shard_map/psum | solution.py:145
  642.6 30.0 %psum.51 = f32[16,16]{1,0:T(8,128)S(1)} all-reduce(f32[16,16]{1,0:T(8,128)S(1)} %convolution_bitcast_fusion.18), channel_id=1, replica_groups=mesh['groups'=2,'slab'=16] {'slab'}, use_global_device_ids=true, to_apply=%region_11.13 | all-reduce | flops 256 | bytes 2048 | tf_op jit(solution)/shard_map/psum | solution.py:148
  672.7 24.4 %while.141 = (s32[]{:T(128)}, f32[16,16]{1,0:T(8,128)S(1)}, f32[16,16]{0,1:T(8,128)S(1)}, s32[]{:T(128)}, s32[]{:T(128)}) while((s32[]{:T(128)}, f32[16,16]{1,0:T(8,128)S(1)}, f32[16,16]{0,1:T(8,128)S(1)}, s32[]{:T(128)}, s32[]{:T(128)}) %tuple.551), condition=%wide.region_13.15_spmd.clone.clone, body=%wide.region_12.14_spmd.clone.clone.sunk | while | flops 3955 | bytes 14736 | solution.py:68
  697.1 34.1 %while.142 = (s32[]{:T(128)}, f32[16,16]{1,0:T(8,128)S(1)}, f32[16,16]{1,0:T(8,128)}, f32[16,16]{1,0:T(8,128)S(1)}, s32[]{:T(128)}, /*index=5*/s32[]{:T(128)}, s32[]{:T(128)}) while((s32[]{:T(128)}, f32[16,16]{1,0:T(8,128)S(1)}, f32[16,16]{1,0:T(8,128)}, f32[16,16]{1,0:T(8,128)S(1)}, s32[]{:T(128)}, ...), condition=%wide.region_15.17_spmd.clone.clone, body=%wide.region_14.16_spmd.clone.clone.sunk | while | flops 3924 | bytes 13155 | solution.py:86
  734.2 57.9 %psum.52 = f32[32,16]{1,0:T(8,128)S(1)} all-reduce(f32[32,16]{1,0:T(8,128)S(1)} %convolution_bitcast_fusion.15), channel_id=1, replica_groups=mesh['groups'=2,'slab'=16] {'slab'}, use_global_device_ids=true, to_apply=%region_16.18 | all-reduce | flops 512 | bytes 4096 | tf_op jit(solution)/shard_map/psum | solution.py:145
  803.9 30.0 %psum.53 = f32[16,16]{1,0:T(8,128)S(1)} all-reduce(f32[16,16]{1,0:T(8,128)S(1)} %convolution_bitcast_fusion.17), channel_id=1, replica_groups=mesh['groups'=2,'slab'=16] {'slab'}, use_global_device_ids=true, to_apply=%region_17.19 | all-reduce | flops 256 | bytes 2048 | tf_op jit(solution)/shard_map/psum | solution.py:148
  834.0 24.4 %while.143 = (s32[]{:T(128)}, f32[16,16]{1,0:T(8,128)S(1)}, f32[16,16]{0,1:T(8,128)S(1)}, s32[]{:T(128)}, s32[]{:T(128)}) while((s32[]{:T(128)}, f32[16,16]{1,0:T(8,128)S(1)}, f32[16,16]{0,1:T(8,128)S(1)}, s32[]{:T(128)}, s32[]{:T(128)}) %tuple.550), condition=%wide.region_19.21_spmd.clone.clone, body=%wide.region_18.20_spmd.clone.clone.sunk | while | flops 3955 | bytes 14736 | solution.py:68
  858.4 34.1 %while.144 = (s32[]{:T(128)}, f32[16,16]{1,0:T(8,128)S(1)}, f32[16,16]{1,0:T(8,128)}, f32[16,16]{1,0:T(8,128)S(1)}, s32[]{:T(128)}, /*index=5*/s32[]{:T(128)}, s32[]{:T(128)}) while((s32[]{:T(128)}, f32[16,16]{1,0:T(8,128)S(1)}, f32[16,16]{1,0:T(8,128)}, f32[16,16]{1,0:T(8,128)S(1)}, s32[]{:T(128)}, ...), condition=%wide.region_21.23_spmd.clone.clone, body=%wide.region_20.22_spmd.clone.clone.sunk | while | flops 3924 | bytes 13155 | solution.py:86
  896.0 57.6 %psum.54 = f32[48,16]{1,0:T(8,128)S(1)} all-reduce(f32[48,16]{1,0:T(8,128)S(1)} %fusion.90), channel_id=1, replica_groups=mesh['groups'=2,'slab'=16] {'slab'}, use_global_device_ids=true, to_apply=%region_22.24 | all-reduce | flops 768 | bytes 6144 | tf_op jit(solution)/shard_map/psum | solution.py:145
  962.0 30.0 %psum.55 = f32[16,16]{1,0:T(8,128)S(1)} all-reduce(f32[16,16]{1,0:T(8,128)S(1)} %convolution_bitcast_fusion.16), channel_id=1, replica_groups=mesh['groups'=2,'slab'=16] {'slab'}, use_global_device_ids=true, to_apply=%region_23.25 | all-reduce | flops 256 | bytes 2048 | tf_op jit(solution)/shard_map/psum | solution.py:148
  992.1 24.4 %while.145 = (s32[]{:T(128)}, f32[16,16]{1,0:T(8,128)S(1)}, f32[16,16]{0,1:T(8,128)S(1)}, s32[]{:T(128)}, s32[]{:T(128)}) while((s32[]{:T(128)}, f32[16,16]{1,0:T(8,128)S(1)}, f32[16,16]{0,1:T(8,128)S(1)}, s32[]{:T(128)}, s32[]{:T(128)}) %tuple.549), condition=%wide.region_25.27_spmd.clone.clone, body=%wide.region_24.26_spmd.clone.clone.sunk | while | flops 3955 | bytes 14736 | solution.py:68
  1016.6 34.1 %while.146 = (s32[]{:T(128)}, f32[16,16]{1,0:T(8,128)S(1)}, f32[16,16]{1,0:T(8,128)}, f32[16,16]{1,0:T(8,128)S(1)}, s32[]{:T(128)}, /*index=5*/s32[]{:T(128)}, s32[]{:T(128)}) while((s32[]{:T(128)}, f32[16,16]{1,0:T(8,128)S(1)}, f32[16,16]{1,0:T(8,128)}, f32[16,16]{1,0:T(8,128)S(1)}, s32[]{:T(128)}, ...), condition=%wide.region_27.29_spmd.clone.clone, body=%wide.region_26.28_spmd.clone.clone.sunk | while | flops 3924 | bytes 13155 | solution.py:86
  (1295 shorter events, 438.7 us)
Async XLA Ops:
  8.1 33.1 %all-to-all-start.1 = ((f32[16,64,1]{1,2,0:T(1,128)}), f32[16,64,1]{1,2,0:T(1,128)S(1)}, u32[]{:S(2)}, u32[]{:S(2)}) async-start(f32[16,64,1]{1,2,0:T(1,128)} %bitcast.16), calls=%async_computation.1 | async-start | bytes 16384 | tf_op jit(solution)/shard_map/all_to_all | solution.py:114
  41.8 38.2 %all-to-all-start = ((f32[16,64,320]{2,1,0:T(8,128)}), f32[16,64,320]{2,1,0:T(8,128)S(1)}, u32[]{:S(2)}, u32[]{:S(2)}) async-start(f32[16,64,320]{2,1,0:T(8,128)} %bitcast.14), calls=%async_computation | async-start | bytes 3145728 | tf_op jit(solution)/shard_map/all_to_all | solution.py:113
  51.6 223.7 %copy-start.129 = (f32[1,1,2048]{2,1,0:T(1,128)}, f32[1,1,2048]{2,1,0:T(1,128)S(1)}, u32[]{:S(2)}) copy-start(f32[1,1,2048]{2,1,0:T(1,128)S(1)} %get-tuple-element.1472) | copy-start | bytes 24580
  51.8 224.3 %copy-start.121 = (f32[1,1,2048]{2,1,0:T(1,128)}, f32[1,1,2048]{2,1,0:T(1,128)S(1)}, u32[]{:S(2)}) copy-start(f32[1,1,2048]{2,1,0:T(1,128)S(1)} %get-tuple-element.1462) | copy-start | bytes 24580
  51.8 224.3 %copy-start.123 = (f32[1,1,2048]{2,1,0:T(1,128)}, f32[1,1,2048]{2,1,0:T(1,128)S(1)}, u32[]{:S(2)}) copy-start(f32[1,1,2048]{2,1,0:T(1,128)S(1)} %get-tuple-element.1463) | copy-start | bytes 24580
  51.8 224.3 %copy-start.125 = (f32[1,1,2048]{2,1,0:T(1,128)}, f32[1,1,2048]{2,1,0:T(1,128)S(1)}, u32[]{:S(2)}) copy-start(f32[1,1,2048]{2,1,0:T(1,128)S(1)} %get-tuple-element.1464) | copy-start | bytes 24580
  51.8 224.3 %copy-start.127 = (f32[1,1,2048]{2,1,0:T(1,128)}, f32[1,1,2048]{2,1,0:T(1,128)S(1)}, u32[]{:S(2)}) copy-start(f32[1,1,2048]{2,1,0:T(1,128)S(1)} %get-tuple-element.1465) | copy-start | bytes 24580
  51.8 224.5 %copy-start.111 = (f32[1,1,2048]{2,1,0:T(1,128)}, f32[1,1,2048]{2,1,0:T(1,128)S(1)}, u32[]{:S(2)}) copy-start(f32[1,1,2048]{2,1,0:T(1,128)S(1)} %get-tuple-element.1457) | copy-start | bytes 24580
  51.8 224.5 %copy-start.113 = (f32[1,1,2048]{2,1,0:T(1,128)}, f32[1,1,2048]{2,1,0:T(1,128)S(1)}, u32[]{:S(2)}) copy-start(f32[1,1,2048]{2,1,0:T(1,128)S(1)} %get-tuple-element.1458) | copy-start | bytes 24580
  51.8 224.5 %copy-start.115 = (f32[1,1,2048]{2,1,0:T(1,128)}, f32[1,1,2048]{2,1,0:T(1,128)S(1)}, u32[]{:S(2)}) copy-start(f32[1,1,2048]{2,1,0:T(1,128)S(1)} %get-tuple-element.1459) | copy-start | bytes 24580
  51.8 224.5 %copy-start.117 = (f32[1,1,2048]{2,1,0:T(1,128)}, f32[1,1,2048]{2,1,0:T(1,128)S(1)}, u32[]{:S(2)}) copy-start(f32[1,1,2048]{2,1,0:T(1,128)S(1)} %get-tuple-element.1460) | copy-start | bytes 24580
  51.8 224.5 %copy-start.119 = (f32[1,1,2048]{2,1,0:T(1,128)}, f32[1,1,2048]{2,1,0:T(1,128)S(1)}, u32[]{:S(2)}) copy-start(f32[1,1,2048]{2,1,0:T(1,128)S(1)} %get-tuple-element.1461) | copy-start | bytes 24580
  51.9 224.7 %copy-start.101 = (f32[1,1,2048]{2,1,0:T(1,128)}, f32[1,1,2048]{2,1,0:T(1,128)S(1)}, u32[]{:S(2)}) copy-start(f32[1,1,2048]{2,1,0:T(1,128)S(1)} %get-tuple-element.1452) | copy-start | bytes 24580
  51.9 224.7 %copy-start.103 = (f32[1,1,2048]{2,1,0:T(1,128)}, f32[1,1,2048]{2,1,0:T(1,128)S(1)}, u32[]{:S(2)}) copy-start(f32[1,1,2048]{2,1,0:T(1,128)S(1)} %get-tuple-element.1453) | copy-start | bytes 24580
  51.9 224.7 %copy-start.105 = (f32[1,1,2048]{2,1,0:T(1,128)}, f32[1,1,2048]{2,1,0:T(1,128)S(1)}, u32[]{:S(2)}) copy-start(f32[1,1,2048]{2,1,0:T(1,128)S(1)} %get-tuple-element.1454) | copy-start | bytes 24580
  51.9 224.7 %copy-start.107 = (f32[1,1,2048]{2,1,0:T(1,128)}, f32[1,1,2048]{2,1,0:T(1,128)S(1)}, u32[]{:S(2)}) copy-start(f32[1,1,2048]{2,1,0:T(1,128)S(1)} %get-tuple-element.1455) | copy-start | bytes 24580
  51.9 224.7 %copy-start.109 = (f32[1,1,2048]{2,1,0:T(1,128)}, f32[1,1,2048]{2,1,0:T(1,128)S(1)}, u32[]{:S(2)}) copy-start(f32[1,1,2048]{2,1,0:T(1,128)S(1)} %get-tuple-element.1456) | copy-start | bytes 24580
  51.9 225.0 %copy-start.91 = (f32[1,1,2048]{2,1,0:T(1,128)}, f32[1,1,2048]{2,1,0:T(1,128)S(1)}, u32[]{:S(2)}) copy-start(f32[1,1,2048]{2,1,0:T(1,128)S(1)} %get-tuple-element.1447) | copy-start | bytes 24580
  51.9 225.0 %copy-start.93 = (f32[1,1,2048]{2,1,0:T(1,128)}, f32[1,1,2048]{2,1,0:T(1,128)S(1)}, u32[]{:S(2)}) copy-start(f32[1,1,2048]{2,1,0:T(1,128)S(1)} %get-tuple-element.1448) | copy-start | bytes 24580
  51.9 225.0 %copy-start.95 = (f32[1,1,2048]{2,1,0:T(1,128)}, f32[1,1,2048]{2,1,0:T(1,128)S(1)}, u32[]{:S(2)}) copy-start(f32[1,1,2048]{2,1,0:T(1,128)S(1)} %get-tuple-element.1449) | copy-start | bytes 24580
  51.9 225.0 %copy-start.97 = (f32[1,1,2048]{2,1,0:T(1,128)}, f32[1,1,2048]{2,1,0:T(1,128)S(1)}, u32[]{:S(2)}) copy-start(f32[1,1,2048]{2,1,0:T(1,128)S(1)} %get-tuple-element.1450) | copy-start | bytes 24580
  51.9 225.0 %copy-start.99 = (f32[1,1,2048]{2,1,0:T(1,128)}, f32[1,1,2048]{2,1,0:T(1,128)S(1)}, u32[]{:S(2)}) copy-start(f32[1,1,2048]{2,1,0:T(1,128)S(1)} %get-tuple-element.1451) | copy-start | bytes 24580
  52.1 225.5 %copy-start.83 = (f32[1,1,2048]{2,1,0:T(1,128)}, f32[1,1,2048]{2,1,0:T(1,128)S(1)}, u32[]{:S(2)}) copy-start(f32[1,1,2048]{2,1,0:T(1,128)S(1)} %get-tuple-element.1437) | copy-start | bytes 24580
  52.1 225.5 %copy-start.85 = (f32[1,1,2048]{2,1,0:T(1,128)}, f32[1,1,2048]{2,1,0:T(1,128)S(1)}, u32[]{:S(2)}) copy-start(f32[1,1,2048]{2,1,0:T(1,128)S(1)} %get-tuple-element.1438) | copy-start | bytes 24580
  52.1 225.5 %copy-start.87 = (f32[1,1,2048]{2,1,0:T(1,128)}, f32[1,1,2048]{2,1,0:T(1,128)S(1)}, u32[]{:S(2)}) copy-start(f32[1,1,2048]{2,1,0:T(1,128)S(1)} %get-tuple-element.1439) | copy-start | bytes 24580
  52.1 225.5 %copy-start.89 = (f32[1,1,2048]{2,1,0:T(1,128)}, f32[1,1,2048]{2,1,0:T(1,128)S(1)}, u32[]{:S(2)}) copy-start(f32[1,1,2048]{2,1,0:T(1,128)S(1)} %get-tuple-element.1440) | copy-start | bytes 24580
  52.1 225.8 %copy-start.79 = (f32[1,1,2048]{2,1,0:T(1,128)}, f32[1,1,2048]{2,1,0:T(1,128)S(1)}, u32[]{:S(2)}) copy-start(f32[1,1,2048]{2,1,0:T(1,128)S(1)} %get-tuple-element.1435) | copy-start | bytes 24580
  52.1 225.8 %copy-start.81 = (f32[1,1,2048]{2,1,0:T(1,128)}, f32[1,1,2048]{2,1,0:T(1,128)S(1)}, u32[]{:S(2)}) copy-start(f32[1,1,2048]{2,1,0:T(1,128)S(1)} %get-tuple-element.1436) | copy-start | bytes 24580
  88.5 5.1 collective-permute-start
  91.2 5.0 collective-permute-start.1
  291.8 10.5 collective-permute-start.2
  299.1 3.5 collective-permute-start.3
  (193 other events, 4023.8 us)
where the time goes:
time: 1070 us; the launch traced here: 1050 us
  local copies, waits for them, and re-layouts  451 us (42%)
  blocking collectives  273 us (26%)
  matrix products  127 us (12%)
  other arithmetic  98.8 us (9%)
  loops' own time  45.6 us (4%)
  waiting for transfers between devices  30 us (3%)
  starting transfers between devices  26.2 us (2%)
    gather x24, local copies, waits for them, and re-layouts, local(): gathered = jnp.take(padded, local_ids[slot_index], axis=2)  310 us
    psum x3, blocking collectives, local(): projection = lax.psum(gram_matrix(previous, panel_cols), 'slab')  146 us
    psum x4, blocking collectives, local(): lax.psum(gram_matrix(panel_cols, panel_cols), 'slab')  128 us
    dot_general x64, matrix products, row_step(): jnp.dot(earlier, inverse, precision=lax.Precision.HIGHEST)  93.2 us
    another operation x4, loops' own time, cholesky_upper(): lax.fori_loop(0, order, column_step, jnp.zeros((order, order), jnp.float32))  45.1 us
    dynamic_slice x64, local copies, waits for them, and re-layouts, column_step(): lax.dynamic_index_in_dim(reduced, column_at, 0, keepdims=False)  38 us
    dynamic_slice x64, local copies, waits for them, and re-layouts, row_step(): pivot = lax.dynamic_index_in_dim(lower_row, row_at, 0, keepdims=False)  37.7 us
    unnamed x68, other arithmetic  29.4 us
  transfers between devices with their start and end apart: 6, of which 3 were waited for; matrix products, arithmetic and copies ran while one was open for 3% of the time, Pallas kernels for 0%

commit v1 on v0

--- a/solution.py
+++ b/solution.py
@@ -145,7 +145,9 @@
             projection = lax.psum(gram_matrix(previous, panel_cols), "slab")
             panel_cols = panel_cols - combine(projection, previous)
             factor = factor.at[:start_col, start_col : start_col + block_width].set(projection)
-        diag_block = cholesky_upper(lax.psum(gram_matrix(panel_cols, panel_cols), "slab"))
+        diag_block = cholesky_upper(
+            jnp.sum(lax.all_gather(gram_matrix(panel_cols, panel_cols), "slab"), axis=0)
+        )
         factor = factor.at[
             start_col : start_col + block_width, start_col : start_col + block_width
         ].set(diag_block)

time: 1070 us -> 1020 us (0.953)
  blocking collectives: 273 us -> 230 us
    psum x4 -> x0, blocking collectives: 128 us -> none  [local(): lax.psum(gram_matrix(panel_cols, panel_cols), 'slab')]
    all_gather x0 -> x4, blocking collectives: none -> 80.7 us  [local(): lax.all_gather(gram_matrix(panel_cols, panel_cols), 'slab')]
where the time goes in v1:
time: 1020 us; the launch traced here: 1010 us
  local copies, waits for them, and re-layouts  451 us (44%)
  blocking collectives  230 us (23%)
  matrix products  127 us (12%)
  other arithmetic  98.9 us (10%)
  loops' own time  45.6 us (4%)
  waiting for transfers between devices  30 us (3%)
  starting transfers between devices  26.2 us (3%)
    gather x24, local copies, waits for them, and re-layouts, local(): gathered = jnp.take(padded, local_ids[slot_index], axis=2)  310 us
    psum x3, blocking collectives, local(): projection = lax.psum(gram_matrix(previous, panel_cols), 'slab')  150 us
    dot_general x64, matrix products, row_step(): jnp.dot(earlier, inverse, precision=lax.Precision.HIGHEST)  93.2 us
    all_gather x4, blocking collectives, local(): lax.all_gather(gram_matrix(panel_cols, panel_cols), 'slab')  80.7 us
    another operation x4, loops' own time, cholesky_upper(): lax.fori_loop(0, order, column_step, jnp.zeros((order, order), jnp.float32))  45.1 us
    dynamic_slice x64, local copies, waits for them, and re-layouts, column_step(): lax.dynamic_index_in_dim(reduced, column_at, 0, keepdims=False)  38 us
    dynamic_slice x64, local copies, waits for them, and re-layouts, row_step(): pivot = lax.dynamic_index_in_dim(lower_row, row_at, 0, keepdims=False)  37.7 us
    unnamed x68, other arithmetic  29.4 us
  transfers between devices with their start and end apart: 6, of which 3 were waited for; matrix products, arithmetic and copies ran while one was open for 3% of the time, Pallas kernels for 0%

profile of v1, /device:TPU:0, one launch (start us, length us, event | category | flops | bytes accessed | tf_op | source)
XLA Modules:
  0.0 1012.0 jit_solution(14904849575668290291)
XLA Ops:
  8.1 7.4 all-to-all-start.1
  52.9 27.0 %all-to-all-done = f32[16,64,320]{2,1,0:T(8,128)S(1)} async-done(((f32[16,64,320]{2,1,0:T(8,128)}), f32[16,64,320]{2,1,0:T(8,128)S(1)}, u32[]{:S(2)}, u32[]{:S(2)}) %all-to-all-start) | async-done | bytes 1310752 | tf_op jit(solution)/shard_map/all_to_all | solution.py:113
  98.3 7.6 copy.118
  105.9 19.7 %gather_fusion.5 = f32[2048,5,64]{2,1,0:T(8,128)} fusion(f32[5,64,2561]{1,0,2:T(8,128)} %copy.118, s32[2048]{0:T(1024)} %get-tuple-element.1532), kind=kCustom, calls=%fused_computation.5.clone | custom fusion | bytes 5251072 | tf_op jit(solution)/shard_map/jit(_take)/gather | solution.py:134
  131.7 19.6 %gather_fusion.4 = f32[2048,5,64]{2,1,0:T(8,128)} fusion(f32[5,64,2561]{1,0,2:T(8,128)} %copy.118, s32[2048]{0:T(1024)S(1)} %copy-done.195), kind=kCustom, calls=%fused_computation.4.clone | custom fusion | bytes 5251072 | tf_op jit(solution)/shard_map/jit(_take)/gather | solution.py:134
  157.4 19.6 %gather_fusion.3 = f32[2048,5,64]{2,1,0:T(8,128)} fusion(f32[5,64,2561]{1,0,2:T(8,128)} %copy.118, s32[2048]{0:T(1024)S(1)} %copy-done.193), kind=kCustom, calls=%fused_computation.3.clone | custom fusion | bytes 5251072 | tf_op jit(solution)/shard_map/jit(_take)/gather | solution.py:134
  183.1 19.6 %gather_fusion.2 = f32[2048,5,64]{2,1,0:T(8,128)} fusion(f32[5,64,2561]{1,0,2:T(8,128)} %copy.118, s32[2048]{0:T(1024)S(1)} %copy-done.198), kind=kCustom, calls=%fused_computation.2.clone | custom fusion | bytes 5251072 | tf_op jit(solution)/shard_map/jit(_take)/gather | solution.py:134
  208.8 19.6 %gather_fusion.1 = f32[2048,5,64]{2,1,0:T(8,128)} fusion(f32[5,64,2561]{1,0,2:T(8,128)} %copy.118, s32[2048]{0:T(1024)S(1)} %copy-done.196), kind=kCustom, calls=%fused_computation.1.clone | custom fusion | bytes 5251072 | tf_op jit(solution)/shard_map/jit(_take)/gather | solution.py:134
  234.5 19.6 %gather_fusion = f32[2048,5,64]{2,1,0:T(8,128)} fusion(f32[5,64,2561]{1,0,2:T(8,128)} %copy.118, s32[2048]{0:T(1024)S(1)} %get-tuple-element.1533), kind=kCustom, calls=%fused_computation.clone | custom fusion | bytes 5251072 | tf_op jit(solution)/shard_map/jit(_take)/gather | solution.py:134
  291.8 7.3 collective-permute-start.2
  304.6 7.6 copy.135
  312.3 19.7 %gather_fusion.11 = f32[2048,5,64]{2,1,0:T(8,128)} fusion(f32[5,64,2561]{1,0,2:T(8,128)} %copy.135, s32[2048]{0:T(1024)} %get-tuple-element.1532), kind=kCustom, calls=%fused_computation.11.clone | custom fusion | bytes 5251072 | tf_op jit(solution)/shard_map/jit(_take)/gather | solution.py:134
  332.0 19.8 %gather_fusion.10 = f32[2048,5,64]{2,1,0:T(8,128)} fusion(f32[5,64,2561]{1,0,2:T(8,128)} %copy.135, s32[2048]{0:T(1024)} %get-tuple-element.1531), kind=kCustom, calls=%fused_computation.10.clone | custom fusion | bytes 5251072 | tf_op jit(solution)/shard_map/jit(_take)/gather | solution.py:134
  351.9 19.7 %gather_fusion.9 = f32[2048,5,64]{2,1,0:T(8,128)} fusion(f32[5,64,2561]{1,0,2:T(8,128)} %copy.135, s32[2048]{0:T(1024)S(1)} %copy-done.194), kind=kCustom, calls=%fused_computation.9.clone | custom fusion | bytes 5251072 | tf_op jit(solution)/shard_map/jit(_take)/gather | solution.py:134
  371.5 19.8 %gather_fusion.8 = f32[2048,5,64]{2,1,0:T(8,128)} fusion(f32[5,64,2561]{1,0,2:T(8,128)} %copy.135, s32[2048]{0:T(1024)} %get-tuple-element.1529), kind=kCustom, calls=%fused_computation.8.clone | custom fusion | bytes 5251072 | tf_op jit(solution)/shard_map/jit(_take)/gather | solution.py:134
  391.4 19.8 %gather_fusion.7 = f32[2048,5,64]{2,1,0:T(8,128)} fusion(f32[5,64,2561]{1,0,2:T(8,128)} %copy.135, s32[2048]{0:T(1024)S(1)} %copy-done.197), kind=kCustom, calls=%fused_computation.7.clone | custom fusion | bytes 5251072 | tf_op jit(solution)/shard_map/jit(_take)/gather | solution.py:134
  411.2 19.7 %gather_fusion.6 = f32[2048,5,64]{2,1,0:T(8,128)} fusion(f32[5,64,2561]{1,0,2:T(8,128)} %copy.135, s32[2048]{0:T(1024)} %copy-done.199), kind=kCustom, calls=%fused_computation.6.clone | custom fusion | bytes 5251072 | tf_op jit(solution)/shard_map/jit(_take)/gather | solution.py:134
  511.8 28.3 %all-gather = f32[256,16]{1,0:T(8,128)S(1)} all-gather(f32[16,16]{1,0:T(8,128)S(1)} %convolution_bitcast_fusion.20), channel_id=2, replica_groups=mesh['groups'=2,'slab'=16] {'slab'}, dimensions={0}, use_global_device_ids=true | all-gather | bytes 17408 | tf_op jit(solution)/shard_map/all_gather | solution.py:149
  540.2 24.4 %while.139 = (s32[]{:T(128)}, f32[16,16]{1,0:T(8,128)S(1)}, f32[16,16]{0,1:T(8,128)S(1)}, s32[]{:T(128)}, s32[]{:T(128)}) while((s32[]{:T(128)}, f32[16,16]{1,0:T(8,128)S(1)}, f32[16,16]{0,1:T(8,128)S(1)}, s32[]{:T(128)}, s32[]{:T(128)}) %tuple.540), condition=%wide.region_7.9_spmd.clone.clone, body=%wide.region_6.8_spmd.clone.clone.sunk | while | flops 3955 | bytes 14736 | solution.py:68
  564.6 34.1 %while.140 = (s32[]{:T(128)}, f32[16,16]{1,0:T(8,128)S(1)}, f32[16,16]{1,0:T(8,128)}, f32[16,16]{1,0:T(8,128)S(1)}, s32[]{:T(128)}, /*index=5*/s32[]{:T(128)}, s32[]{:T(128)}) while((s32[]{:T(128)}, f32[16,16]{1,0:T(8,128)S(1)}, f32[16,16]{1,0:T(8,128)}, f32[16,16]{1,0:T(8,128)S(1)}, s32[]{:T(128)}, ...), condition=%wide.region_9.11_spmd.clone.clone, body=%wide.region_8.10_spmd.clone.clone.sunk | while | flops 3924 | bytes 13155 | solution.py:86
  600.4 30.3 %psum.21 = f32[16,16]{1,0:T(8,128)S(1)} all-reduce(f32[16,16]{1,0:T(8,128)S(1)} %convolution_bitcast_fusion.19), channel_id=1, replica_groups=mesh['groups'=2,'slab'=16] {'slab'}, use_global_device_ids=true, to_apply=%region_10.12 | all-reduce | flops 256 | bytes 2048 | tf_op jit(solution)/shard_map/psum | solution.py:145
  633.5 17.5 %all-gather.1 = f32[256,16]{1,0:T(8,128)S(1)} all-gather(f32[16,16]{1,0:T(8,128)S(1)} %convolution_bitcast_fusion.18), channel_id=3, replica_groups=mesh['groups'=2,'slab'=16] {'slab'}, dimensions={0}, use_global_device_ids=true | all-gather | bytes 17408 | tf_op jit(solution)/shard_map/all_gather | solution.py:149
  651.0 24.4 %while.141 = (s32[]{:T(128)}, f32[16,16]{1,0:T(8,128)S(1)}, f32[16,16]{0,1:T(8,128)S(1)}, s32[]{:T(128)}, s32[]{:T(128)}) while((s32[]{:T(128)}, f32[16,16]{1,0:T(8,128)S(1)}, f32[16,16]{0,1:T(8,128)S(1)}, s32[]{:T(128)}, s32[]{:T(128)}) %tuple.539), condition=%wide.region_13.15_spmd.clone.clone, body=%wide.region_12.14_spmd.clone.clone.sunk | while | flops 3955 | bytes 14736 | solution.py:68
  675.5 34.1 %while.142 = (s32[]{:T(128)}, f32[16,16]{1,0:T(8,128)S(1)}, f32[16,16]{1,0:T(8,128)}, f32[16,16]{1,0:T(8,128)S(1)}, s32[]{:T(128)}, /*index=5*/s32[]{:T(128)}, s32[]{:T(128)}) while((s32[]{:T(128)}, f32[16,16]{1,0:T(8,128)S(1)}, f32[16,16]{1,0:T(8,128)}, f32[16,16]{1,0:T(8,128)S(1)}, s32[]{:T(128)}, ...), condition=%wide.region_15.17_spmd.clone.clone, body=%wide.region_14.16_spmd.clone.clone.sunk | while | flops 3924 | bytes 13155 | solution.py:86
  712.6 59.9 %psum.22 = f32[32,16]{1,0:T(8,128)S(1)} all-reduce(f32[32,16]{1,0:T(8,128)S(1)} %convolution_bitcast_fusion.15), channel_id=1, replica_groups=mesh['groups'=2,'slab'=16] {'slab'}, use_global_device_ids=true, to_apply=%region_16.18 | all-reduce | flops 512 | bytes 4096 | tf_op jit(solution)/shard_map/psum | solution.py:145
  784.4 17.5 %all-gather.2 = f32[256,16]{1,0:T(8,128)S(1)} all-gather(f32[16,16]{1,0:T(8,128)S(1)} %convolution_bitcast_fusion.17), channel_id=4, replica_groups=mesh['groups'=2,'slab'=16] {'slab'}, dimensions={0}, use_global_device_ids=true | all-gather | bytes 17408 | tf_op jit(solution)/shard_map/all_gather | solution.py:149
  802.0 24.4 %while.143 = (s32[]{:T(128)}, f32[16,16]{1,0:T(8,128)S(1)}, f32[16,16]{0,1:T(8,128)S(1)}, s32[]{:T(128)}, s32[]{:T(128)}) while((s32[]{:T(128)}, f32[16,16]{1,0:T(8,128)S(1)}, f32[16,16]{0,1:T(8,128)S(1)}, s32[]{:T(128)}, s32[]{:T(128)}) %tuple.538), condition=%wide.region_19.21_spmd.clone.clone, body=%wide.region_18.20_spmd.clone.clone.sunk | while | flops 3955 | bytes 14736 | solution.py:68
  826.4 34.1 %while.144 = (s32[]{:T(128)}, f32[16,16]{1,0:T(8,128)S(1)}, f32[16,16]{1,0:T(8,128)}, f32[16,16]{1,0:T(8,128)S(1)}, s32[]{:T(128)}, /*index=5*/s32[]{:T(128)}, s32[]{:T(128)}) while((s32[]{:T(128)}, f32[16,16]{1,0:T(8,128)S(1)}, f32[16,16]{1,0:T(8,128)}, f32[16,16]{1,0:T(8,128)S(1)}, s32[]{:T(128)}, ...), condition=%wide.region_21.23_spmd.clone.clone, body=%wide.region_20.22_spmd.clone.clone.sunk | while | flops 3924 | bytes 13155 | solution.py:86
  864.0 59.4 %psum.23 = f32[48,16]{1,0:T(8,128)S(1)} all-reduce(f32[48,16]{1,0:T(8,128)S(1)} %fusion.90), channel_id=1, replica_groups=mesh['groups'=2,'slab'=16] {'slab'}, use_global_device_ids=true, to_apply=%region_22.24 | all-reduce | flops 768 | bytes 6144 | tf_op jit(solution)/shard_map/psum | solution.py:145
  931.8 17.5 %all-gather.3 = f32[256,16]{1,0:T(8,128)S(1)} all-gather(f32[16,16]{1,0:T(8,128)S(1)} %convolution_bitcast_fusion.16), channel_id=5, replica_groups=mesh['groups'=2,'slab'=16] {'slab'}, dimensions={0}, use_global_device_ids=true | all-gather | bytes 17408 | tf_op jit(solution)/shard_map/all_gather | solution.py:149
  949.4 24.4 %while.145 = (s32[]{:T(128)}, f32[16,16]{1,0:T(8,128)S(1)}, f32[16,16]{0,1:T(8,128)S(1)}, s32[]{:T(128)}, s32[]{:T(128)}) while((s32[]{:T(128)}, f32[16,16]{1,0:T(8,128)S(1)}, f32[16,16]{0,1:T(8,128)S(1)}, s32[]{:T(128)}, s32[]{:T(128)}) %tuple.537), condition=%wide.region_25.27_spmd.clone.clone, body=%wide.region_24.26_spmd.clone.clone.sunk | while | flops 3955 | bytes 14736 | solution.py:68
  973.9 34.1 %while.146 = (s32[]{:T(128)}, f32[16,16]{1,0:T(8,128)S(1)}, f32[16,16]{1,0:T(8,128)}, f32[16,16]{1,0:T(8,128)S(1)}, s32[]{:T(128)}, /*index=5*/s32[]{:T(128)}, s32[]{:T(128)}) while((s32[]{:T(128)}, f32[16,16]{1,0:T(8,128)S(1)}, f32[16,16]{1,0:T(8,128)}, f32[16,16]{1,0:T(8,128)S(1)}, s32[]{:T(128)}, ...), condition=%wide.region_27.29_spmd.clone.clone, body=%wide.region_26.28_spmd.clone.clone.sunk | while | flops 3924 | bytes 13155 | solution.py:86
  (1299 shorter events, 438.8 us)
Async XLA Ops:
  8.1 33.1 %all-to-all-start.1 = ((f32[16,64,1]{1,2,0:T(1,128)}), f32[16,64,1]{1,2,0:T(1,128)S(1)}, u32[]{:S(2)}, u32[]{:S(2)}) async-start(f32[16,64,1]{1,2,0:T(1,128)} %bitcast.16), calls=%async_computation.1 | async-start | bytes 16384 | tf_op jit(solution)/shard_map/all_to_all | solution.py:114
  41.8 38.2 %all-to-all-start = ((f32[16,64,320]{2,1,0:T(8,128)}), f32[16,64,320]{2,1,0:T(8,128)S(1)}, u32[]{:S(2)}, u32[]{:S(2)}) async-start(f32[16,64,320]{2,1,0:T(8,128)} %bitcast.14), calls=%async_computation | async-start | bytes 3145728 | tf_op jit(solution)/shard_map/all_to_all | solution.py:113
  51.6 223.7 %copy-start.129 = (f32[1,1,2048]{2,1,0:T(1,128)}, f32[1,1,2048]{2,1,0:T(1,128)S(1)}, u32[]{:S(2)}) copy-start(f32[1,1,2048]{2,1,0:T(1,128)S(1)} %get-tuple-element.1436) | copy-start | bytes 24580
  51.8 224.3 %copy-start.121 = (f32[1,1,2048]{2,1,0:T(1,128)}, f32[1,1,2048]{2,1,0:T(1,128)S(1)}, u32[]{:S(2)}) copy-start(f32[1,1,2048]{2,1,0:T(1,128)S(1)} %get-tuple-element.1426) | copy-start | bytes 24580
  51.8 224.3 %copy-start.123 = (f32[1,1,2048]{2,1,0:T(1,128)}, f32[1,1,2048]{2,1,0:T(1,128)S(1)}, u32[]{:S(2)}) copy-start(f32[1,1,2048]{2,1,0:T(1,128)S(1)} %get-tuple-element.1427) | copy-start | bytes 24580
  51.8 224.3 %copy-start.125 = (f32[1,1,2048]{2,1,0:T(1,128)}, f32[1,1,2048]{2,1,0:T(1,128)S(1)}, u32[]{:S(2)}) copy-start(f32[1,1,2048]{2,1,0:T(1,128)S(1)} %get-tuple-element.1428) | copy-start | bytes 24580
  51.8 224.3 %copy-start.127 = (f32[1,1,2048]{2,1,0:T(1,128)}, f32[1,1,2048]{2,1,0:T(1,128)S(1)}, u32[]{:S(2)}) copy-start(f32[1,1,2048]{2,1,0:T(1,128)S(1)} %get-tuple-element.1429) | copy-start | bytes 24580
  51.8 224.5 %copy-start.111 = (f32[1,1,2048]{2,1,0:T(1,128)}, f32[1,1,2048]{2,1,0:T(1,128)S(1)}, u32[]{:S(2)}) copy-start(f32[1,1,2048]{2,1,0:T(1,128)S(1)} %get-tuple-element.1421) | copy-start | bytes 24580
  51.8 224.5 %copy-start.113 = (f32[1,1,2048]{2,1,0:T(1,128)}, f32[1,1,2048]{2,1,0:T(1,128)S(1)}, u32[]{:S(2)}) copy-start(f32[1,1,2048]{2,1,0:T(1,128)S(1)} %get-tuple-element.1422) | copy-start | bytes 24580
  51.8 224.5 %copy-start.115 = (f32[1,1,2048]{2,1,0:T(1,128)}, f32[1,1,2048]{2,1,0:T(1,128)S(1)}, u32[]{:S(2)}) copy-start(f32[1,1,2048]{2,1,0:T(1,128)S(1)} %get-tuple-element.1423) | copy-start | bytes 24580
  51.8 224.5 %copy-start.117 = (f32[1,1,2048]{2,1,0:T(1,128)}, f32[1,1,2048]{2,1,0:T(1,128)S(1)}, u32[]{:S(2)}) copy-start(f32[1,1,2048]{2,1,0:T(1,128)S(1)} %get-tuple-element.1424) | copy-start | bytes 24580
  51.8 224.5 %copy-start.119 = (f32[1,1,2048]{2,1,0:T(1,128)}, f32[1,1,2048]{2,1,0:T(1,128)S(1)}, u32[]{:S(2)}) copy-start(f32[1,1,2048]{2,1,0:T(1,128)S(1)} %get-tuple-element.1425) | copy-start | bytes 24580
  51.9 224.7 %copy-start.101 = (f32[1,1,2048]{2,1,0:T(1,128)}, f32[1,1,2048]{2,1,0:T(1,128)S(1)}, u32[]{:S(2)}) copy-start(f32[1,1,2048]{2,1,0:T(1,128)S(1)} %get-tuple-element.1416) | copy-start | bytes 24580
  51.9 224.7 %copy-start.103 = (f32[1,1,2048]{2,1,0:T(1,128)}, f32[1,1,2048]{2,1,0:T(1,128)S(1)}, u32[]{:S(2)}) copy-start(f32[1,1,2048]{2,1,0:T(1,128)S(1)} %get-tuple-element.1417) | copy-start | bytes 24580
  51.9 224.7 %copy-start.105 = (f32[1,1,2048]{2,1,0:T(1,128)}, f32[1,1,2048]{2,1,0:T(1,128)S(1)}, u32[]{:S(2)}) copy-start(f32[1,1,2048]{2,1,0:T(1,128)S(1)} %get-tuple-element.1418) | copy-start | bytes 24580
  51.9 224.7 %copy-start.107 = (f32[1,1,2048]{2,1,0:T(1,128)}, f32[1,1,2048]{2,1,0:T(1,128)S(1)}, u32[]{:S(2)}) copy-start(f32[1,1,2048]{2,1,0:T(1,128)S(1)} %get-tuple-element.1419) | copy-start | bytes 24580
  51.9 224.7 %copy-start.109 = (f32[1,1,2048]{2,1,0:T(1,128)}, f32[1,1,2048]{2,1,0:T(1,128)S(1)}, u32[]{:S(2)}) copy-start(f32[1,1,2048]{2,1,0:T(1,128)S(1)} %get-tuple-element.1420) | copy-start | bytes 24580
  51.9 225.0 %copy-start.91 = (f32[1,1,2048]{2,1,0:T(1,128)}, f32[1,1,2048]{2,1,0:T(1,128)S(1)}, u32[]{:S(2)}) copy-start(f32[1,1,2048]{2,1,0:T(1,128)S(1)} %get-tuple-element.1411) | copy-start | bytes 24580
  51.9 225.0 %copy-start.93 = (f32[1,1,2048]{2,1,0:T(1,128)}, f32[1,1,2048]{2,1,0:T(1,128)S(1)}, u32[]{:S(2)}) copy-start(f32[1,1,2048]{2,1,0:T(1,128)S(1)} %get-tuple-element.1412) | copy-start | bytes 24580
  51.9 225.0 %copy-start.95 = (f32[1,1,2048]{2,1,0:T(1,128)}, f32[1,1,2048]{2,1,0:T(1,128)S(1)}, u32[]{:S(2)}) copy-start(f32[1,1,2048]{2,1,0:T(1,128)S(1)} %get-tuple-element.1413) | copy-start | bytes 24580
  51.9 225.0 %copy-start.97 = (f32[1,1,2048]{2,1,0:T(1,128)}, f32[1,1,2048]{2,1,0:T(1,128)S(1)}, u32[]{:S(2)}) copy-start(f32[1,1,2048]{2,1,0:T(1,128)S(1)} %get-tuple-element.1414) | copy-start | bytes 24580
  51.9 225.0 %copy-start.99 = (f32[1,1,2048]{2,1,0:T(1,128)}, f32[1,1,2048]{2,1,0:T(1,128)S(1)}, u32[]{:S(2)}) copy-start(f32[1,1,2048]{2,1,0:T(1,128)S(1)} %get-tuple-element.1415) | copy-start | bytes 24580
  52.1 225.5 %copy-start.83 = (f32[1,1,2048]{2,1,0:T(1,128)}, f32[1,1,2048]{2,1,0:T(1,128)S(1)}, u32[]{:S(2)}) copy-start(f32[1,1,2048]{2,1,0:T(1,128)S(1)} %get-tuple-element.1401) | copy-start | bytes 24580
  52.1 225.5 %copy-start.85 = (f32[1,1,2048]{2,1,0:T(1,128)}, f32[1,1,2048]{2,1,0:T(1,128)S(1)}, u32[]{:S(2)}) copy-start(f32[1,1,2048]{2,1,0:T(1,128)S(1)} %get-tuple-element.1402) | copy-start | bytes 24580
  52.1 225.5 %copy-start.87 = (f32[1,1,2048]{2,1,0:T(1,128)}, f32[1,1,2048]{2,1,0:T(1,128)S(1)}, u32[]{:S(2)}) copy-start(f32[1,1,2048]{2,1,0:T(1,128)S(1)} %get-tuple-element.1403) | copy-start | bytes 24580
  52.1 225.5 %copy-start.89 = (f32[1,1,2048]{2,1,0:T(1,128)}, f32[1,1,2048]{2,1,0:T(1,128)S(1)}, u32[]{:S(2)}) copy-start(f32[1,1,2048]{2,1,0:T(1,128)S(1)} %get-tuple-element.1404) | copy-start | bytes 24580
  52.1 225.8 %copy-start.79 = (f32[1,1,2048]{2,1,0:T(1,128)}, f32[1,1,2048]{2,1,0:T(1,128)S(1)}, u32[]{:S(2)}) copy-start(f32[1,1,2048]{2,1,0:T(1,128)S(1)} %get-tuple-element.1399) | copy-start | bytes 24580
  52.1 225.8 %copy-start.81 = (f32[1,1,2048]{2,1,0:T(1,128)}, f32[1,1,2048]{2,1,0:T(1,128)S(1)}, u32[]{:S(2)}) copy-start(f32[1,1,2048]{2,1,0:T(1,128)S(1)} %get-tuple-element.1400) | copy-start | bytes 24580
  88.5 5.1 collective-permute-start
  91.2 5.0 collective-permute-start.1
  291.8 10.5 %collective-permute-start.2 = (f32[5,64,256]{2,1,0:T(8,128)S(1)}, f32[5,64,256]{2,1,0:T(8,128)S(1)}, u32[]{:S(2)}, u32[]{:S(2)}) collective-permute-start(f32[5,64,256]{2,1,0:T(8,128)S(1)} %get-tuple-element.1323), channel_id=1, source_target_pairs={{0,1},{1,2},{2,3},{3,4},{4,5},{5,6},{6,7},{7,8},{8,9},{9,10},{10,1... | collective-permute-start | bytes 983048 | tf_op jit(solution)/shard_map/ppermute | solution.py:19
  299.1 3.5 collective-permute-start.3
  (193 other events, 3925.0 us)
